TPU v7x, 512 devices: a whole 4x8x8 slice. The times are simulated.
512 devices in a mesh: dp: 16 (over y, z_lo), vocab: 32 (over x, z_hi, core).
Axes of the slice: x: 4, y: 8, z: 8 (z_hi: 4, z_lo: 2; z = z_hi * 2 + z_lo), core: 2. Of those that a mesh axis runs over, the one named last changes fastest.
Arguments:
- hidden: bfloat16 [2048, 3072], P('dp')
- head: bfloat16 [16, 8192, 3072], P('dp', 'vocab')
- teacher: bfloat16 [2048, 131072], P('dp', 'vocab')
- shard_order: int32 [32], replicated, may hold values from 0 to 31, each once
- loss_weight: float32 [2048], replicated, may hold values from 256 to 2048
Outputs:
- head_grad: bfloat16 [16, 8192, 3072], P('dp', 'vocab')
- divergence: float32 [2048], replicated
Inputs may be any that keep to these rules, and one draw needn't show every extreme that they name: `shard_order`: each block number appears once.
All inputs are finite; a program needn't handle non-finite values.
Results may differ from a plain program's by a relative error of at most 0.0048.
Values may be sent and summed in bfloat16 or wider, within the bound.
A program may use at most 128 MiB of HBM per device.

v0:
```python
import jax
import jax.numpy as jnp
from jax import lax
from jax.sharding import PartitionSpec as P


def on_device(hidden, head, teacher, shard_order, loss_weight):
    rows_all = lax.all_gather(hidden, "dp", axis=0, tiled=True)
    rows_head = head[0]
    student = lax.dot_general(
        rows_all, rows_head, (((1,), (1,)), ((), ())), preferred_element_type=jnp.float32
    )
    token_rows = teacher.shape[0]
    vocab_count = lax.axis_size("vocab")
    piece_cols = teacher.shape[1] // vocab_count
    split_view = teacher.reshape(token_rows, vocab_count, piece_cols)
    spread_view = lax.all_to_all(split_view, "vocab", split_axis=1, concat_axis=1, tiled=True)
    ordinal = jnp.arange(vocab_count, dtype=jnp.int32)
    matches = (shard_order[None, :] == ordinal[:, None]).astype(jnp.int32)
    inverse = jnp.sum(matches * ordinal[None, :], axis=1)
    sorted_view = jnp.take(spread_view, inverse, axis=1)
    collected = lax.all_to_all(
        sorted_view, "vocab", split_axis=1, concat_axis=1, tiled=True
    ).reshape(token_rows, vocab_count * piece_cols)
    target = lax.all_to_all(collected, "dp", split_axis=1, concat_axis=0, tiled=True).astype(
        jnp.float32
    )
    top_s, top_t = lax.pmax((jnp.max(student, axis=1), jnp.max(target, axis=1)), ("dp", "vocab"))
    exp_s = jnp.exp(student - top_s[:, None])
    exp_t = jnp.exp(target - top_t[:, None])
    sum_s, sum_t, cross = lax.psum(
        (
            jnp.sum(exp_s, axis=1),
            jnp.sum(exp_t, axis=1),
            jnp.sum(exp_t * (target - student), axis=1),
        ),
        ("dp", "vocab"),
    )
    divergence = cross / sum_t - top_t - jnp.log(sum_t) + top_s + jnp.log(sum_s)
    prob_s = exp_s / sum_s[:, None]
    prob_t = exp_t / sum_t[:, None]
    logit_grad = (loss_weight[:, None] * (prob_s - prob_t)).astype(jnp.bfloat16)
    grad_rows = lax.dot_general(
        logit_grad, rows_all, (((0,), (0,)), ((), ())), preferred_element_type=jnp.float32
    )
    return (grad_rows.astype(jnp.bfloat16)[None], divergence)


def solution(mesh):
    in_specs = (P("dp", None), P("dp", "vocab", None), P("dp", "vocab"), P(), P())
    out_specs = (P("dp", "vocab", None), P())
    return jax.shard_map(
        on_device, mesh=mesh, in_specs=in_specs, out_specs=out_specs, check_vma=False
    )
```

profile of v0, /device:TPU:1, one launch (start us, length us, event | category | flops | bytes accessed | tf_op | source)
XLA Modules:
  0.0 561.9 jit_solution(18264371202213001680)
XLA Ops:
  7.2 0.0 copy-start
  7.2 0.0 all-gather.2.cloned.1.call-start
  7.2 0.7 all-gather.2.cloned.1.call-update
  7.9 1.6 copy.13
  9.5 0.0 copy-start.2
  9.6 1.3 copy.14
  10.9 14.5 %all-to-all-start = ((bf16[128,32,128]{2,0,1:T(8,128)(2,1)}), bf16[128,32,128]{2,0,1:T(8,128)(2,1)}, u32[]{:S(2)}, u32[]{:S(2)}) async-start(bf16[128,32,128]{2,0,1:T(8,128)(2,1)} %copy.14), calls=%async_computation | async-start | bytes 2097152 | tf_op jit(solution)/shard_map/all_to_all | solution.py:17
  25.4 0.0 copy-done.2
  25.4 0.1 select_reduce_fusion
  25.5 52.1 %all-to-all-done = bf16[128,32,128]{2,0,1:T(8,128)(2,1)} async-done(((bf16[128,32,128]{2,0,1:T(8,128)(2,1)}), bf16[128,32,128]{2,0,1:T(8,128)(2,1)}, u32[]{:S(2)}, u32[]{:S(2)}) %all-to-all-start) | async-done | bytes 1048608 | tf_op jit(solution)/shard_map/all_to_all | solution.py:17
  77.6 2.0 gather_fusion
  79.6 0.2 select_bitcast_fusion
  79.8 59.9 %all_to_all.26 = bf16[128,32,128]{2,0,1:T(8,128)(2,1)S(1)} all-to-all(bf16[128,32,128]{2,0,1:T(8,128)(2,1)S(1)} %select_bitcast_fusion), channel_id=1, replica_groups=mesh['dp'=16,'vocab'=32] {'vocab'}, dimensions={1} | all-to-all | bytes 2097152 | tf_op jit(solution)/shard_map/all_to_all | solution.py:22
  139.7 1.3 copy.15
  141.0 46.4 %all_to_all.27 = bf16[128,16,256]{0,2,1:T(8,128)(2,1)S(1)} all-to-all(bf16[128,16,256]{0,2,1:T(8,128)(2,1)} %bitcast.48), channel_id=1, replica_groups=mesh['dp'=16,'vocab'=32] {'dp'}, dimensions={1} | all-to-all | bytes 2097152 | tf_op jit(solution)/shard_map/all_to_all | solution.py:25
  187.4 0.2 bitcast_reduce_fusion
  187.5 150.1 %all-gather.2.cloned.1.call-done = bf16[2048,3072]{1,0:T(8,128)(2,1)} async-done(((bf16[128,3072]{1,0:T(8,128)(2,1)}), bf16[2048,3072]{1,0:T(8,128)(2,1)}) %all-gather.2.cloned.1.call-update) | async-done | bytes 12582928 | tf_op jit(solution)/shard_map/all_gather | solution.py:8
  337.7 0.0 copy-done
  337.7 9.4 %fusion.15 = (f32[2048]{0:T(1024)S(1)}, f32[2048,256]{0,1:T(8,128)}) fusion(bf16[2048,3072]{1,0:T(8,128)(2,1)} %all-gather.2.cloned.1.call-done, bf16[1,256,3072]{2,1,0:T(8,128)(2,1)S(1)} %copy-done), kind=kOutput, calls=%fused_computation.33 | convolution fusion | flops 3221747712 | bytes 16261120 | tf_op jit(solution)/shard_map/dot_general | solution.py:10
  347.0 99.3 %all-reduce.1 = (f32[2048]{0:T(1024)S(1)}, f32[2048]{0:T(1024)S(1)}) all-reduce(f32[2048]{0:T(1024)S(1)} %bitcast_convert_fusion, f32[2048]{0:T(1024)S(1)} %get-tuple-element.9), channel_id=1, replica_groups=mesh['dp'=16,'vocab'=32] {'dp','vocab'}, use_global_device_ids=true, to_apply=%region_6.7 | all-reduce | flops 4096 | bytes 32768 | tf_op jit(solution)/shard_map/pmax | solution.py:28
  446.3 0.0 copy-start.1
  446.3 0.4 fusion.2
  446.7 2.4 fusion.5
  449.0 95.4 %all-reduce = (f32[2048]{0:T(1024)S(1)}, f32[2048]{0:T(1024)S(1)}, f32[2048]{0:T(1024)S(1)}) all-reduce(f32[2048]{0:T(1024)S(1)} %bitcast.51, f32[2048]{0:T(1024)S(1)} %get-tuple-element.3, f32[2048]{0:T(1024)S(1)} %get-tuple-element.2), channel_id=1, replica_groups=mesh['dp'=16,'vocab'=32] {'dp','vocab'}, use_global_device_ids=true, to_apply=%region_8.9 | all-reduce | flops 6144 | bytes 49152 | tf_op jit(solution)/shard_map/psum | solution.py:31
  544.4 0.6 log_add_fusion
  545.0 0.0 copy-done.1
  545.0 10.1 %fusion = bf16[1,256,3072]{2,1,0:T(8,128)(2,1)} fusion(bf16[2048,3072]{1,0:T(8,128)(2,1)} %all-gather.2.cloned.1.call-done, f32[2048,256]{0,1:T(8,128)} %get-tuple-element.10, f32[2048]{0:T(1024)S(1)} %get-tuple-element.4, f32[2048]{0:T(1024)S(1)} %get-tuple-element.7, f32[2048]{0:T(1024)S(1)} %get-tuple-element.5, f32[2048]{0:T(1024)S(1)} %get-tuple-element.8, ...), kind=kOutput, calls=%fused_computation.2 | convolution fusion | flops 3226206208 | bytes 17342464 | tf_op jit(solution)/shard_map/dot_general | solution.py:43
  (4 shorter events, 0.0 us)
Async XLA Ops:
  7.2 330.5 %copy-start = (bf16[1,256,3072]{2,1,0:T(8,128)(2,1)S(1)}, bf16[1,256,3072]{2,1,0:T(8,128)(2,1)}, u32[]{:S(2)}) copy-start(bf16[1,256,3072]{2,1,0:T(8,128)(2,1)} %param.6) | copy-start | bytes 4718596
  7.2 330.5 %all-gather.2.cloned.1.call-start = ((), (), s32[]{:S(2)}) async-start(), calls=%async_computation.3 | async-start | bytes 13369344 | tf_op jit(solution)/shard_map/all_gather | solution.py:8
  9.5 15.8 %copy-start.2 = (s32[32]{0:T(128)S(1)}, s32[32]{0:T(128)}, u32[]{:S(2)}) copy-start(s32[32]{0:T(128)} %param.8) | copy-start | bytes 388
  10.9 66.8 %all-to-all-start = ((bf16[128,32,128]{2,0,1:T(8,128)(2,1)}), bf16[128,32,128]{2,0,1:T(8,128)(2,1)}, u32[]{:S(2)}, u32[]{:S(2)}) async-start(bf16[128,32,128]{2,0,1:T(8,128)(2,1)} %copy.14), calls=%async_computation | async-start | bytes 2097152 | tf_op jit(solution)/shard_map/all_to_all | solution.py:17
  446.3 98.7 %copy-start.1 = (f32[2048]{0:T(1024)S(1)}, f32[2048]{0:T(1024)}, u32[]{:S(2)}) copy-start(f32[2048]{0:T(1024)} %param.9) | copy-start | bytes 24580
Sparse Core Ops, SparseCore 0:
  10.1 327.5 all-gather.1
where the time goes:
time: 562 us
  blocking collectives  301 us (54%)
  waiting for transfers between devices  203 us (36%)
  matrix products  19.5 us (3%)
  starting transfers between devices  14.5 us (3%)
  between operations  14.1 us (3%)
  local copies, waits for them, and re-layouts  6.22 us (1%)
    all_gather x1, waiting for transfers between devices, on_device(): rows_all = lax.all_gather(hidden, 'dp', axis=0, tiled=True)  150 us
    pmax x1, blocking collectives, on_device(): lax.pmax((jnp.max(student, axis=1), jnp.max(target, axis=1)), ('dp', 'voc...  99.3 us
    psum x1, blocking collectives, on_device(): lax.psum((jnp.sum(exp_s, axis=1), jnp.sum(exp_t, axis=1), jnp.sum(exp_t *...  95.4 us
    all_to_all x1, blocking collectives, on_device(): lax.all_to_all(sorted_view, 'vocab', split_axis=1, concat_axis=1, tiled=T...  59.9 us
    all_to_all x1, waiting for transfers between devices, on_device(): lax.all_to_all(split_view, 'vocab', split_axis=1, concat_axis=1, tiled=True)  52.1 us
    all_to_all x1, blocking collectives, on_device(): lax.all_to_all(collected, 'dp', split_axis=1, concat_axis=0, tiled=True)  46.4 us
    all_to_all x1, starting transfers between devices, on_device(): lax.all_to_all(split_view, 'vocab', split_axis=1, concat_axis=1, tiled=True)  14.5 us
  transfers between devices with their start and end apart: 2, of which 2 were waited for; matrix products, arithmetic and copies ran while one was open for 1% of the time, Pallas kernels for 0%

commit v1 on v0

v1 whole, which is shorter than its diff:
```python
import functools

import jax
import jax.numpy as jnp
from jax import lax
from jax.experimental import pallas as pl
from jax.experimental.pallas import tpu as pltpu
from jax.sharding import PartitionSpec as P

F32 = jnp.float32
BF16 = jnp.bfloat16
MESH = pl.DeviceIdType.MESH
SUB = 256


def kernel(
    nx, ny, nzh,
    inv_ref, hidden_ref, head_hbm, teacher_hbm, weight_ref,
    grad_ref, div_ref,
    hid, head, tv, tt, rr, qq, ww, tgt, sc, ex, pr,
    src1, ar1, tile2, ar2, tile3, fin, tst,
    csrc1, car1, ctile2, car2, ctile3, cfin,
    loc, zs, zr, ys, yr, xs, xr, cs, cr, t1s, t1r, t2s, t2r, t3s, t3r, as_, ar_,
):
    half = ny // 2
    n_dp = 2 * ny
    n_v = 2 * nx * nzh
    d_model = hid.shape[-1]
    me_s = lax.axis_index("dp")
    me_v = lax.axis_index("vocab")
    y, zl = me_s // 2, me_s % 2
    x, c = me_v // (2 * nzh), me_v % 2
    xp = x % 2
    other = 2 * y + 1 - zl
    y_nbr = [{"dp": ((y + 1) % ny) * 2 + zl}, {"dp": ((y + ny - 1) % ny) * 2 + zl}]
    x_nbr = [
        {"vocab": ((x + 1) % nx) * (2 * nzh) + me_v % (2 * nzh)},
        {"vocab": ((x + nx - 1) % nx) * (2 * nzh) + me_v % (2 * nzh)},
    ]
    sib = {"vocab": me_v + 1 - 2 * c}
    z_peer = {"dp": other}
    base = xp * 64 + c * 32
    obase = (1 - xp) * 64 + c * 32
    base_sib = xp * 64 + (1 - c) * 32
    obase_sib = (1 - xp) * 64 + (1 - c) * 32

    def rows(start, count):
        return pl.ds(pl.multiple_of(start, 16), count)

    def reg2(yb, start, count):
        return hid.at[pl.ds(2 * yb, 2), rows(start, count), :]

    def reg1(s, start, count):
        return hid.at[s, rows(start, count), :]

    def wait(ref, sem):
        pltpu.make_async_copy(ref, ref, sem).wait()

    sent = []

    def send(src, dst, ssem, rsem, dev):
        copy = pltpu.make_async_remote_copy(
            src_ref=src, dst_ref=dst, send_sem=ssem, recv_sem=rsem,
            device_id=dev, device_id_type=MESH,
        )
        copy.start()
        sent.append((src, ssem))

    def send_quiet(src, dst, ssem, rsem, dev):
        pltpu.make_async_remote_copy(
            src_ref=src, dst_ref=dst, send_sem=ssem, recv_sem=rsem,
            device_id=dev, device_id_type=MESH,
        ).start()

    own = pltpu.make_async_copy(hidden_ref, hid.at[me_s], loc.at[0])
    own.start()
    tload = pltpu.make_async_copy(teacher_hbm, tv, loc.at[1])
    tload.start()
    hload = pltpu.make_async_copy(head_hbm, head, loc.at[2])
    hload.start()

    barrier = pltpu.get_barrier_semaphore()

    def greet_dp(i, _):
        pl.semaphore_signal(
            barrier, inc=1, device_id={"dp": (me_s + i) % n_dp}, device_id_type=MESH
        )
        return 0

    def greet_v(i, _):
        pl.semaphore_signal(
            barrier, inc=1, device_id={"vocab": (me_v + i) % n_v}, device_id_type=MESH
        )
        return 0

    lax.fori_loop(1, n_dp, greet_dp, 0)
    lax.fori_loop(1, n_v, greet_v, 0)
    pl.semaphore_wait(barrier, n_dp + n_v - 2)

    send(hidden_ref.at[rows(base, 32), :], reg1(me_s, base, 32), zs.at[0], zr.at[0], z_peer)

    def first_rows(g):
        return (base, 32) if half > 1 else (base + 16 * g, 16)

    for g in range(2):
        st, ct = first_rows(g)
        send(hidden_ref.at[rows(st, ct), :], reg1(me_s, st, ct),
             ys.at[g, 0], yr.at[g, 0], y_nbr[g])

    tload.wait()

    def t1_step(i, _):
        s = (me_s + i) % n_dp
        cols = pl.ds(pl.multiple_of(s * SUB, SUB), SUB)
        block = jnp.transpose(tv[:, cols])
        tt[2 * s] = block[:128]
        tt[2 * s + 1] = block[128:]
        send_quiet(tt.at[pl.ds(2 * s, 2)], rr.at[pl.ds(2 * me_s, 2)],
                   t1s.at[0], t1r.at[me_s], {"dp": s})
        return 0

    lax.fori_loop(1, n_dp, t1_step, 0)
    own_block = jnp.transpose(tv[:, pl.ds(pl.multiple_of(me_s * SUB, SUB), SUB)])
    tt[2 * me_s] = own_block[:128]
    tt[2 * me_s + 1] = own_block[128:]
    rr[2 * me_s] = own_block[:128]
    rr[2 * me_s + 1] = own_block[128:]

    def t2_step(s):
        for h in range(2):
            k = 2 * s + h

            @pl.when(k != me_v)
            def _():
                send_quiet(rr.at[k], qq.at[me_v], t2s.at[0], t2r.at[0], {"vocab": k})

            @pl.when(k == me_v)
            def _():
                qq[me_v] = rr[k]

    def t2_range(lo, hi):
        def body(i, _):
            s = (me_s + n_dp - i) % n_dp
            wait(rr.at[pl.ds(2 * s, 2)], t1r.at[s])
            t2_step(s)
            return 0

        lax.fori_loop(lo, hi, body, 0)

    def t3_all():
        wait(qq.at[pl.ds(0, n_v - 1)], t2r.at[0])

        def body(j, _):
            v = (me_v + j) % n_v
            ww[v] = qq[inv_ref[v]]
            send_quiet(ww.at[v], tgt.at[me_v], t3s.at[0], t3r.at[0], {"vocab": v})
            return 0

        lax.fori_loop(1, n_v, body, 0)
        tgt[me_v] = qq[inv_ref[me_v]]

    row_id = lax.broadcasted_iota(jnp.int32, (8, 128), 0)

    def as_tile(parts):
        tile = jnp.zeros((8, 128), F32)
        for r, part in enumerate(parts):
            tile = jnp.where(row_id == r, part, tile)
        return tile

    def teacher_stats():
        def mx(i, acc):
            return jnp.maximum(acc, tt[i].astype(F32))

        top = lax.fori_loop(1, n_v, mx, tt[0].astype(F32))
        top = jnp.max(top, axis=0, keepdims=True)

        def sm(i, acc):
            return acc + jnp.exp(tt[i].astype(F32) - top)

        total = lax.fori_loop(0, n_v, sm, jnp.zeros((128, 128), F32))
        total = jnp.sum(total, axis=0, keepdims=True)
        tst[...] = as_tile([top, total])

    def block_y(idx):
        d = (idx + 1) // 2
        return (y + ny - d) % ny if idx % 2 == 1 else (y + d) % ny

    def send_x(idx, q):
        yb = block_y(idx)
        part = reg1(other, base + 16 * q, 16) if idx == 0 else reg2(yb, base + 16 * q, 16)
        send(part, part, xs.at[q, idx], xr.at[q, idx], x_nbr[q])

    def send_core(idx, kind):
        yb = block_y(idx)
        st = base if kind == 0 else obase
        part = reg1(other, st, 32) if idx == 0 else reg2(yb, st, 32)
        send(part, part, cs.at[kind, idx], cr.at[kind, idx], sib)

    def y_recv(idx):
        yb = block_y(idx)
        d = (idx + 1) // 2
        if idx == 0:
            wait(reg1(other, base, 32), zr.at[0])
            for g in range(2):
                st, ct = first_rows(g)
                part = reg1(other, st, ct)
                send(part, part, ys.at[g, 1], yr.at[g, 1], y_nbr[g])
            for q in range(2):
                send_x(idx, q)
        elif d < half:
            g = 0 if idx % 2 == 1 else 1
            if d == 1:
                wait(reg1(2 * yb + zl, base, 32), yr.at[g, 0])
                wait(reg1(2 * yb + 1 - zl, base, 32), yr.at[g, 1])
            for q in ((0, 1) if g == 0 else (1, 0)):
                if d > 1:
                    wait(reg2(yb, base + 16 * q, 16), yr.at[g, 2 * (d - 1) + q])
                if d + 1 < half or q == g:
                    part = reg2(yb, base + 16 * q, 16)
                    send(part, part, ys.at[g, 2 * d + q], yr.at[g, 2 * d + q], y_nbr[g])
                send_x(idx, q)
        else:
            for g in range(2):
                if d == 1:
                    wait(reg1(2 * yb + zl, base + 16 * g, 16), yr.at[g, 0])
                    wait(reg1(2 * yb + 1 - zl, base + 16 * g, 16), yr.at[g, 1])
                else:
                    wait(reg2(yb, base + 16 * g, 16), yr.at[g, 2 * (d - 1) + g])
                send_x(idx, g)
        send_core(idx, 0)

    def x_recv(idx):
        yb = block_y(idx)
        for q in range(2):
            part = reg1(other, obase + 16 * q, 16) if idx == 0 else reg2(yb, obase + 16 * q, 16)
            wait(part, xr.at[q, idx])
        send_core(idx, 1)

    def compute(idx):
        yb = block_y(idx)
        for kind in range(2):
            st = base_sib if kind == 0 else obase_sib
            part = reg1(other, st, 32) if idx == 0 else reg2(yb, st, 32)
            wait(part, cr.at[kind, idx])
        block = hid[pl.ds(2 * yb, 2)].reshape(256, d_model)
        scores = lax.dot_general(
            head[...], block, (((1,), (1,)), ((), ())), preferred_element_type=F32
        )
        cols = pl.ds(pl.multiple_of(yb * 256, 256), 256)
        sc[:, cols] = scores
        top = jnp.max(scores, axis=0, keepdims=True)
        e = jnp.exp(scores - top)
        ex[:, cols] = e
        total = jnp.sum(e, axis=0, keepdims=True)
        for j in range(2):
            lanes = slice(128 * j, 128 * j + 128)
            src1[2 * yb + j] = as_tile([top[:, lanes], total[:, lanes]])

    own.wait()
    hload.wait()
    t2_step(me_s)
    t2_plan = {1: (1, 3), 2: (3, 7), 3: (7, 12), 4: (12, n_dp)}
    t3_stage = 6
    t2_done, t3_done = 1, False
    for stage in range(ny + 2):
        if stage < ny:
            y_recv(stage)
        if stage == 0:
            teacher_stats()
        if stage in t2_plan:
            lo, hi = t2_plan[stage]
            lo, hi = min(lo, n_dp), min(hi, n_dp)
            if hi > lo:
                t2_range(lo, hi)
            t2_done = hi
        if 1 <= stage <= ny:
            x_recv(stage - 1)
        if stage >= 2:
            compute(stage - 2)
        if stage == t3_stage:
            t3_all()
            t3_done = True
    if t2_done < n_dp:
        t2_range(t2_done, n_dp)
    if not t3_done:
        t3_all()

    def spread_dp(src, dst, k):
        def body(i, _):
            s = (me_s + i) % n_dp
            send_quiet(src.at[s], dst.at[me_s], as_.at[k], ar_.at[k], {"dp": s})
            return 0

        lax.fori_loop(1, n_dp, body, 0)
        dst[me_s] = src[me_s]

    def share_v(tile, dst, k):
        def body(i, _):
            send_quiet(tile, dst.at[me_v], as_.at[k], ar_.at[k], {"vocab": (me_v + i) % n_v})
            return 0

        lax.fori_loop(1, n_v, body, 0)
        dst[me_v] = tile[...]

    def share_dp(tile, dst, k):
        def body(i, _):
            send_quiet(tile, dst.at[me_s], as_.at[k], ar_.at[k], {"dp": (me_s + i) % n_dp})
            return 0

        lax.fori_loop(1, n_dp, body, 0)
        dst[me_s] = tile[...]

    def merge(ref, r):
        tops = ref[:, r, :]
        sums = ref[:, r + 1, :]
        top = jnp.max(tops, axis=0, keepdims=True)
        return top, jnp.sum(sums * jnp.exp(tops - top), axis=0, keepdims=True)

    spread_dp(src1, ar1, 0)
    wait(ar1.at[pl.ds(0, n_dp - 1)], ar_.at[0])
    top, total = merge(ar1, 0)
    tile2[...] = as_tile([top, total, tst[0:1, :], tst[1:2, :]])
    share_v(tile2, ar2, 1)
    wait(ar2.at[pl.ds(0, n_v - 1)], ar_.at[1])
    top, total = merge(ar2, 0)
    t_top, t_total = merge(ar2, 2)
    tile3[...] = as_tile([top, total, t_top, t_total])
    share_dp(tile3, fin, 2)
    wait(fin.at[pl.ds(0, n_dp - 1)], ar_.at[2])

    wait(tgt.at[pl.ds(0, n_v - 1)], t3r.at[0])

    def grad_chunk(s, _):
        cols = pl.ds(pl.multiple_of(s * 128, 128), 128)
        f = fin[s]
        m_s, z_s, m_t, z_t = f[0:1], f[1:2], f[2:3], f[3:4]
        w = weight_ref[s]
        scale_s = w * jnp.exp(src1[s][0:1] - m_s) / z_s
        scale_t = w / z_t
        cross = jnp.zeros((1, 128), F32)
        for h in range(2):
            t = tgt[2 * s + h].astype(F32)
            e_t = jnp.exp(t - m_t)
            band = slice(128 * h, 128 * h + 128)
            cross = cross + jnp.sum(e_t * (t - sc[band, cols]), axis=0, keepdims=True)
            pr[band, cols] = (ex[band, cols] * scale_s - e_t * scale_t).astype(BF16)
        csrc1[s] = as_tile([cross])
        return 0

    lax.fori_loop(0, n_dp, grad_chunk, 0)

    n_tiles = d_model // 256

    def gemm(lo, hi):
        def body(n, _):
            cols = pl.ds(pl.multiple_of(n * 256, 256), 256)
            b = hid[:, :, cols].reshape(n_dp * 128, 256)
            grad_ref[:, cols] = jnp.dot(pr[...], b, preferred_element_type=F32).astype(BF16)
            return 0

        lax.fori_loop(lo, hi, body, 0)

    cut1, cut2 = n_tiles // 3, 2 * n_tiles // 3
    spread_dp(csrc1, car1, 3)
    gemm(0, cut1)
    wait(car1.at[pl.ds(0, n_dp - 1)], ar_.at[3])
    ctile2[...] = jnp.sum(car1[...], axis=0)
    share_v(ctile2, car2, 4)
    gemm(cut1, cut2)
    wait(car2.at[pl.ds(0, n_v - 1)], ar_.at[4])
    ctile3[...] = jnp.sum(car2[...], axis=0)
    share_dp(ctile3, cfin, 5)
    gemm(cut2, n_tiles)
    wait(cfin.at[pl.ds(0, n_dp - 1)], ar_.at[5])
    m_s, z_s, m_t, z_t = fin[:, 0, :], fin[:, 1, :], fin[:, 2, :], fin[:, 3, :]
    div_ref[...] = cfin[:, 0, :] / z_t - m_t - jnp.log(z_t) + m_s + jnp.log(z_s)

    for ref, sem in sent:
        wait(ref, sem)
    wait(tt.at[pl.ds(0, 2 * (n_dp - 1))], t1s.at[0])
    wait(rr.at[pl.ds(0, n_v - 1)], t2s.at[0])
    wait(ww.at[pl.ds(0, n_v - 1)], t3s.at[0])
    for k, ref in ((0, ar1), (1, ar2), (2, fin), (3, car1), (4, car2), (5, cfin)):
        wait(ref.at[pl.ds(0, (n_v if k % 3 == 1 else n_dp) - 1)], as_.at[k])


def on_device(nx, ny, nzh, hidden, head, teacher, shard_order, loss_weight):
    n_dp, n_v = 2 * ny, 2 * nx * nzh
    d_model = hidden.shape[1]
    tokens = n_dp * 128
    ordinal = jnp.arange(n_v, dtype=jnp.int32)
    matches = (shard_order[None, :] == ordinal[:, None]).astype(jnp.int32)
    inverse = jnp.sum(matches * ordinal[None, :], axis=1)
    any_ = pl.BlockSpec(memory_space=pl.ANY)
    vmem = pl.BlockSpec(memory_space=pltpu.VMEM)
    smem = pl.BlockSpec(memory_space=pltpu.SMEM)
    dma = pltpu.SemaphoreType.DMA

    def stat(n):
        return pltpu.VMEM((n, 8, 128), F32)

    tile = pltpu.VMEM((8, 128), F32)
    pieces = pltpu.VMEM((n_v, 128, 128), BF16)
    grad, div = pl.pallas_call(
        functools.partial(kernel, nx, ny, nzh),
        out_shape=(
            jax.ShapeDtypeStruct((SUB, d_model), BF16),
            jax.ShapeDtypeStruct((n_dp, 128), F32),
        ),
        in_specs=[smem, any_, any_, any_, vmem],
        out_specs=(vmem, vmem),
        scratch_shapes=[
            pltpu.VMEM((n_dp, 128, d_model), BF16),
            pltpu.VMEM((SUB, d_model), BF16),
            pltpu.VMEM((128, n_dp * SUB), BF16),
            pieces, pieces, pieces, pieces, pieces,
            pltpu.VMEM((SUB, tokens), F32),
            pltpu.VMEM((SUB, tokens), F32),
            pltpu.VMEM((SUB, tokens), BF16),
            stat(n_dp), stat(n_dp), tile, stat(n_v), tile, stat(n_dp), tile,
            stat(n_dp), stat(n_dp), tile, stat(n_v), tile, stat(n_dp),
            dma((3,)),
            dma((1,)), dma((1,)),
            dma((2, ny)), dma((2, ny)),
            dma((2, ny)), dma((2, ny)),
            dma((2, ny)), dma((2, ny)),
            dma((1,)), dma((n_dp,)),
            dma((1,)), dma((1,)),
            dma((1,)), dma((1,)),
            dma((6,)), dma((6,)),
        ],
        compiler_params=pltpu.CompilerParams(
            collective_id=0, has_side_effects=True, vmem_limit_bytes=56 * 1024 * 1024
        ),
        cost_estimate=pl.CostEstimate(
            flops=4 * SUB * tokens * d_model, bytes_accessed=8 * SUB * d_model, transcendentals=0
        ),
    )(inverse, hidden, head[0], teacher, loss_weight.reshape(n_dp, 1, 128))
    return grad[None], div.reshape(tokens)


def build(mesh, nx, ny, nzh):
    in_specs = (P("dp", None), P("dp", "vocab", None), P("dp", "vocab"), P(), P())
    out_specs = (P("dp", "vocab", None), P())
    return jax.shard_map(
        functools.partial(on_device, nx, ny, nzh),
        mesh=mesh, in_specs=in_specs, out_specs=out_specs, check_vma=False,
    )


def solution(mesh):
    return build(mesh, 4, mesh.shape["dp"] // 2, mesh.shape["vocab"] // 8)
```

time: 562 us -> 159 us (0.28)
  blocking collectives: 301 us -> 0 us
  waiting for transfers between devices: 203 us -> 0 us
  Pallas kernels: 0 us -> 154 us
  matrix products: 19.5 us -> 0 us
  starting transfers between devices: 14.5 us -> 0 us
  between operations: 14.1 us -> 0.65 us
    pallas_call x0 -> x1, Pallas kernels: none -> 154 us  [on_device(): pl.pallas_call(functools.partial(kernel, nx, ny, nzh), out_shape=(jax.Sha...]
    all_gather x1 -> x0, waiting for transfers between devices: 150 us -> none  [on_device(): rows_all = lax.all_gather(hidden, 'dp', axis=0, tiled=True)]
    all_to_all x2 -> x0, blocking collectives: 106 us -> none  [the longest x1 59.9 us: on_device(): lax.all_to_all(sorted_view, 'vocab', split_axis=1, concat_axis=1, tiled=T...]
    pmax x1 -> x0, blocking collectives: 99.3 us -> none  [on_device(): lax.pmax((jnp.max(student, axis=1), jnp.max(target, axis=1)), ('dp', 'voc...]
    psum x1 -> x0, blocking collectives: 95.4 us -> none  [on_device(): lax.psum((jnp.sum(exp_s, axis=1), jnp.sum(exp_t, axis=1), jnp.sum(exp_t *...]
    all_to_all x1 -> x0, waiting for transfers between devices: 52.1 us -> none  [on_device(): lax.all_to_all(split_view, 'vocab', split_axis=1, concat_axis=1, tiled=True)]
    dot_general x2 -> x0, matrix products: 19.5 us -> none  [the longest x1 10.1 us: on_device(): lax.dot_general(logit_grad, rows_all, (((0,), (0,)), ((), ())), preferred...]
    all_to_all x1 -> x0, starting transfers between devices: 14.5 us -> none  [on_device(): lax.all_to_all(split_view, 'vocab', split_axis=1, concat_axis=1, tiled=True)]
  transfers between devices with their start and end apart: 2 -> 0, of which waited for: 2 -> 0; matrix products, arithmetic and copies ran while one was open for 1% -> 0% of each run, Pallas kernels for 0% -> 0%
where the time goes in v1:
time: 159 us
  Pallas kernels  154 us (97%)
  local copies, waits for them, and re-layouts  3.26 us (2%)
    pallas_call x1, Pallas kernels, on_device(): pl.pallas_call(functools.partial(kernel, nx, ny, nzh), out_shape=(jax.Sha...  154 us
    unnamed x4, local copies, waits for them, and re-layouts  3.26 us

profile of v1, /device:TPU:1, one launch (start us, length us, event | category | flops | bytes accessed | tf_op | source)
XLA Modules:
  0.0 158.7 jit_solution(11055656983691143213)
XLA Ops:
  0.6 1.3 select_reduce_fusion.inv_ref
  1.9 153.5 %shard_map.68 = (bf16[256,3072]{1,0:T(8,128)(2,1)}, f32[16,128]{1,0:T(8,128)}) custom-call(s32[32]{0:T(128)} %select_reduce_fusion.inv_ref, bf16[128,3072]{1,0:T(8,128)(2,1)} %hidden_ref.1, bf16[256,3072]{1,0:T(8,128)(2,1)} %bitcast.6, bf16[128,4096]{1,0:T(8,128)(2,1)} %teacher_hbm.1, f32[16,1,128]{2,1,0:T(1,128)} %bitcast.7), custom_call_target="tpu_custom_call" | custom-call | flops 6442450944 | bytes 6291456 | tf_op jit(solution)/shard_map/pallas_call | solution.py:404
  155.5 0.0 copy-start
  155.5 2.7 %copy.9 = bf16[1,256,3072]{2,1,0:T(8,128)(2,1)} copy(bf16[1,256,3072]{2,1,0:T(8,128)(2,1)} %bitcast.4) | data formatting | bytes 3145728
  158.1 0.0 copy-done
  158.1 0.6 copy.10
Async XLA Ops:
  155.5 2.7 %copy-start = (f32[16,128]{1,0:T(8,128)S(1)}, f32[16,128]{1,0:T(8,128)}, u32[]{:S(2)}) copy-start(f32[16,128]{1,0:T(8,128)} %get-tuple-element.5) | copy-start | bytes 24580

commit v2 on v1

--- a/solution.py
+++ b/solution.py
@@ -15,10 +15,10 @@
 
 def kernel(
     nx, ny, nzh,
-    inv_ref, hidden_ref, head_hbm, teacher_hbm, weight_ref,
+    order_ref, hidden_ref, head_hbm, teacher_hbm, weight_ref,
     grad_ref, div_ref,
-    hid, head, tv, tt, rr, qq, ww, tgt, sc, ex, pr,
-    src1, ar1, tile2, ar2, tile3, fin, tst,
+    inv, hid, head, tv, tt, rr, qq, ww, tgt, sc, ex, pr,
+    src1, ar1, tile2, ar2, tile3, fin,
     csrc1, car1, ctile2, car2, ctile3, cfin,
     loc, zs, zr, ys, yr, xs, xr, cs, cr, t1s, t1r, t2s, t2r, t3s, t3r, as_, ar_,
 ):
@@ -95,6 +95,13 @@
 
     lax.fori_loop(1, n_dp, greet_dp, 0)
     lax.fori_loop(1, n_v, greet_v, 0)
+    tload.wait()
+
+    def flip(k, _):
+        tt[k] = jnp.transpose(tv[:, pl.ds(pl.multiple_of(k * 128, 128), 128)])
+        return 0
+
+    lax.fori_loop(0, n_v, flip, 0)
     pl.semaphore_wait(barrier, n_dp + n_v - 2)
 
     send(hidden_ref.at[rows(base, 32), :], reg1(me_s, base, 32), zs.at[0], zr.at[0], z_peer)
@@ -107,65 +114,68 @@
         send(hidden_ref.at[rows(st, ct), :], reg1(me_s, st, ct),
              ys.at[g, 0], yr.at[g, 0], y_nbr[g])
 
-    tload.wait()
-
-    def t1_step(i, _):
-        s = (me_s + i) % n_dp
-        cols = pl.ds(pl.multiple_of(s * SUB, SUB), SUB)
-        block = jnp.transpose(tv[:, cols])
-        tt[2 * s] = block[:128]
-        tt[2 * s + 1] = block[128:]
-        send_quiet(tt.at[pl.ds(2 * s, 2)], rr.at[pl.ds(2 * me_s, 2)],
-                   t1s.at[0], t1r.at[me_s], {"dp": s})
-        return 0
-
-    lax.fori_loop(1, n_dp, t1_step, 0)
-    own_block = jnp.transpose(tv[:, pl.ds(pl.multiple_of(me_s * SUB, SUB), SUB)])
-    tt[2 * me_s] = own_block[:128]
-    tt[2 * me_s + 1] = own_block[128:]
-    rr[2 * me_s] = own_block[:128]
-    rr[2 * me_s + 1] = own_block[128:]
-
-    def t2_step(s):
-        for h in range(2):
-            k = 2 * s + h
-
-            @pl.when(k != me_v)
-            def _():
-                send_quiet(rr.at[k], qq.at[me_v], t2s.at[0], t2r.at[0], {"vocab": k})
-
-            @pl.when(k == me_v)
-            def _():
-                qq[me_v] = rr[k]
-
-    def t2_range(lo, hi):
-        def body(i, _):
-            s = (me_s + n_dp - i) % n_dp
-            wait(rr.at[pl.ds(2 * s, 2)], t1r.at[s])
-            t2_step(s)
-            return 0
-
-        lax.fori_loop(lo, hi, body, 0)
+    def t2_step(j, _):
+        k = (me_v + j) % n_v
+        send_quiet(tt.at[k], qq.at[me_v], t2s.at[0], t2r.at[0], {"vocab": k})
+        return 0
+
+    lax.fori_loop(1, n_v, t2_step, 0)
+    qq[me_v] = tt[me_v]
+
+    def inverse_of(v, _):
+        found = order_ref[0] * 0
+        for b in range(n_v):
+            found = jnp.maximum(found, jnp.where(order_ref[b] == v, b, 0))
+        inv[v] = found
+        return 0
+
+    lax.fori_loop(0, n_v, inverse_of, 0)
+    my_pair = me_v // 2
 
     def t3_all():
         wait(qq.at[pl.ds(0, n_v - 1)], t2r.at[0])
 
         def body(j, _):
-            v = (me_v + j) % n_v
-            ww[v] = qq[inv_ref[v]]
-            send_quiet(ww.at[v], tgt.at[me_v], t3s.at[0], t3r.at[0], {"vocab": v})
-            return 0
-
-        lax.fori_loop(1, n_v, body, 0)
-        tgt[me_v] = qq[inv_ref[me_v]]
-
-    row_id = lax.broadcasted_iota(jnp.int32, (8, 128), 0)
-
-    def as_tile(parts):
-        tile = jnp.zeros((8, 128), F32)
-        for r, part in enumerate(parts):
-            tile = jnp.where(row_id == r, part, tile)
-        return tile
+            vp = (j + me_s + n_dp - my_pair) % n_dp
+            for cc in range(2):
+                v = 2 * vp + cc
+
+                @pl.when(v != me_v)
+                def _():
+                    ww[v] = qq[inv[v]]
+                    send_quiet(ww.at[v], rr.at[me_v], t3s.at[0], t3r.at[me_v], {"vocab": v})
+
+                @pl.when(v == me_v)
+                def _():
+                    rr[v] = qq[inv[v]]
+
+            return 0
+
+        lax.fori_loop(0, n_dp, body, 0)
+
+    def t1_range(lo, hi):
+        def body(j, _):
+            s = (j + me_s + n_dp - my_pair) % n_dp
+            for cc in range(2):
+                k = 2 * s + cc
+
+                @pl.when(k != me_v)
+                def _():
+                    wait(rr.at[k], t3r.at[k])
+
+            @pl.when(s != me_s)
+            def _():
+                send_quiet(rr.at[pl.ds(2 * s, 2)], tgt.at[pl.ds(2 * me_s, 2)],
+                           t1s.at[0], t1r.at[0], {"dp": s})
+
+            @pl.when(s == me_s)
+            def _():
+                tgt[2 * s] = rr[2 * s]
+                tgt[2 * s + 1] = rr[2 * s + 1]
+
+            return 0
+
+        lax.fori_loop(lo, hi, body, 0)
 
     def teacher_stats():
         def mx(i, acc):
@@ -178,8 +188,8 @@
             return acc + jnp.exp(tt[i].astype(F32) - top)
 
         total = lax.fori_loop(0, n_v, sm, jnp.zeros((128, 128), F32))
-        total = jnp.sum(total, axis=0, keepdims=True)
-        tst[...] = as_tile([top, total])
+        tile2[2:3, :] = top
+        tile2[3:4, :] = jnp.sum(total, axis=0, keepdims=True)
 
     def block_y(idx):
         d = (idx + 1) // 2
@@ -254,36 +264,26 @@
         total = jnp.sum(e, axis=0, keepdims=True)
         for j in range(2):
             lanes = slice(128 * j, 128 * j + 128)
-            src1[2 * yb + j] = as_tile([top[:, lanes], total[:, lanes]])
+            src1[2 * yb + j, 0:1, :] = top[:, lanes]
+            src1[2 * yb + j, 1:2, :] = total[:, lanes]
 
     own.wait()
     hload.wait()
-    t2_step(me_s)
-    t2_plan = {1: (1, 3), 2: (3, 7), 3: (7, 12), 4: (12, n_dp)}
-    t3_stage = 6
-    t2_done, t3_done = 1, False
+    t1_plan = {ny - 1: (0, 3), ny: (3, 6), ny + 1: (6, 9)}
     for stage in range(ny + 2):
         if stage < ny:
             y_recv(stage)
         if stage == 0:
             teacher_stats()
-        if stage in t2_plan:
-            lo, hi = t2_plan[stage]
-            lo, hi = min(lo, n_dp), min(hi, n_dp)
-            if hi > lo:
-                t2_range(lo, hi)
-            t2_done = hi
         if 1 <= stage <= ny:
             x_recv(stage - 1)
         if stage >= 2:
             compute(stage - 2)
-        if stage == t3_stage:
+        if stage == max(ny - 2, 0):
             t3_all()
-            t3_done = True
-    if t2_done < n_dp:
-        t2_range(t2_done, n_dp)
-    if not t3_done:
-        t3_all()
+        if stage in t1_plan:
+            lo, hi = t1_plan[stage]
+            t1_range(min(lo, n_dp), min(hi, n_dp))
 
     def spread_dp(src, dst, k):
         def body(i, _):
@@ -317,18 +317,18 @@
         return top, jnp.sum(sums * jnp.exp(tops - top), axis=0, keepdims=True)
 
     spread_dp(src1, ar1, 0)
+    t1_range(min(9, n_dp), min(12, n_dp))
     wait(ar1.at[pl.ds(0, n_dp - 1)], ar_.at[0])
-    top, total = merge(ar1, 0)
-    tile2[...] = as_tile([top, total, tst[0:1, :], tst[1:2, :]])
+    tile2[0:1, :], tile2[1:2, :] = merge(ar1, 0)
     share_v(tile2, ar2, 1)
+    t1_range(min(12, n_dp), n_dp)
     wait(ar2.at[pl.ds(0, n_v - 1)], ar_.at[1])
-    top, total = merge(ar2, 0)
-    t_top, t_total = merge(ar2, 2)
-    tile3[...] = as_tile([top, total, t_top, t_total])
+    tile3[0:1, :], tile3[1:2, :] = merge(ar2, 0)
+    tile3[2:3, :], tile3[3:4, :] = merge(ar2, 2)
     share_dp(tile3, fin, 2)
     wait(fin.at[pl.ds(0, n_dp - 1)], ar_.at[2])
 
-    wait(tgt.at[pl.ds(0, n_v - 1)], t3r.at[0])
+    wait(tgt.at[pl.ds(0, n_v - 2)], t1r.at[0])
 
     def grad_chunk(s, _):
         cols = pl.ds(pl.multiple_of(s * 128, 128), 128)
@@ -344,7 +344,7 @@
             band = slice(128 * h, 128 * h + 128)
             cross = cross + jnp.sum(e_t * (t - sc[band, cols]), axis=0, keepdims=True)
             pr[band, cols] = (ex[band, cols] * scale_s - e_t * scale_t).astype(BF16)
-        csrc1[s] = as_tile([cross])
+        csrc1[s] = cross
         return 0
 
     lax.fori_loop(0, n_dp, grad_chunk, 0)
@@ -377,8 +377,8 @@
 
     for ref, sem in sent:
         wait(ref, sem)
-    wait(tt.at[pl.ds(0, 2 * (n_dp - 1))], t1s.at[0])
-    wait(rr.at[pl.ds(0, n_v - 1)], t2s.at[0])
+    wait(tt.at[pl.ds(0, n_v - 1)], t2s.at[0])
+    wait(rr.at[pl.ds(0, n_v - 2)], t1s.at[0])
     wait(ww.at[pl.ds(0, n_v - 1)], t3s.at[0])
     for k, ref in ((0, ar1), (1, ar2), (2, fin), (3, car1), (4, car2), (5, cfin)):
         wait(ref.at[pl.ds(0, (n_v if k % 3 == 1 else n_dp) - 1)], as_.at[k])
@@ -388,18 +388,15 @@
     n_dp, n_v = 2 * ny, 2 * nx * nzh
     d_model = hidden.shape[1]
     tokens = n_dp * 128
-    ordinal = jnp.arange(n_v, dtype=jnp.int32)
-    matches = (shard_order[None, :] == ordinal[:, None]).astype(jnp.int32)
-    inverse = jnp.sum(matches * ordinal[None, :], axis=1)
     any_ = pl.BlockSpec(memory_space=pl.ANY)
     vmem = pl.BlockSpec(memory_space=pltpu.VMEM)
     smem = pl.BlockSpec(memory_space=pltpu.SMEM)
     dma = pltpu.SemaphoreType.DMA
 
-    def stat(n):
-        return pltpu.VMEM((n, 8, 128), F32)
-
-    tile = pltpu.VMEM((8, 128), F32)
+    def stat(n, r):
+        return pltpu.VMEM((n, r, 128), F32)
+
+    tile4, tile1 = pltpu.VMEM((4, 128), F32), pltpu.VMEM((1, 128), F32)
     pieces = pltpu.VMEM((n_v, 128, 128), BF16)
     grad, div = pl.pallas_call(
         functools.partial(kernel, nx, ny, nzh),
@@ -410,6 +407,7 @@
         in_specs=[smem, any_, any_, any_, vmem],
         out_specs=(vmem, vmem),
         scratch_shapes=[
+            pltpu.SMEM((n_v,), jnp.int32),
             pltpu.VMEM((n_dp, 128, d_model), BF16),
             pltpu.VMEM((SUB, d_model), BF16),
             pltpu.VMEM((128, n_dp * SUB), BF16),
@@ -417,16 +415,16 @@
             pltpu.VMEM((SUB, tokens), F32),
             pltpu.VMEM((SUB, tokens), F32),
             pltpu.VMEM((SUB, tokens), BF16),
-            stat(n_dp), stat(n_dp), tile, stat(n_v), tile, stat(n_dp), tile,
-            stat(n_dp), stat(n_dp), tile, stat(n_v), tile, stat(n_dp),
+            stat(n_dp, 2), stat(n_dp, 2), tile4, stat(n_v, 4), tile4, stat(n_dp, 4),
+            stat(n_dp, 1), stat(n_dp, 1), tile1, stat(n_v, 1), tile1, stat(n_dp, 1),
             dma((3,)),
             dma((1,)), dma((1,)),
             dma((2, ny)), dma((2, ny)),
             dma((2, ny)), dma((2, ny)),
             dma((2, ny)), dma((2, ny)),
-            dma((1,)), dma((n_dp,)),
             dma((1,)), dma((1,)),
             dma((1,)), dma((1,)),
+            dma((1,)), dma((n_v,)),
             dma((6,)), dma((6,)),
         ],
         compiler_params=pltpu.CompilerParams(
@@ -435,7 +433,7 @@
         cost_estimate=pl.CostEstimate(
             flops=4 * SUB * tokens * d_model, bytes_accessed=8 * SUB * d_model, transcendentals=0
         ),
-    )(inverse, hidden, head[0], teacher, loss_weight.reshape(n_dp, 1, 128))
+    )(shard_order, hidden, head[0], teacher, loss_weight.reshape(n_dp, 1, 128))
     return grad[None], div.reshape(tokens)
 
 

time: 159 us -> 146 us (0.918)
  Pallas kernels: 154 us -> 142 us
    pallas_call x1, Pallas kernels: 154 us -> 142 us  [on_device(): pl.pallas_call(functools.partial(kernel, nx, ny, nzh), out_shape=(jax.Sha...]
where the time goes in v2:
time: 146 us
  Pallas kernels  142 us (97%)
  local copies, waits for them, and re-layouts  3.26 us (2%)
    pallas_call x1, Pallas kernels, on_device(): pl.pallas_call(functools.partial(kernel, nx, ny, nzh), out_shape=(jax.Sha...  142 us
    unnamed x4, local copies, waits for them, and re-layouts  3.26 us

profile of v2, /device:TPU:1, one launch (start us, length us, event | category | flops | bytes accessed | tf_op | source)
XLA Modules:
  0.0 146.1 jit_solution(18365214510518555906)
XLA Ops:
  0.6 142.2 %shard_map.68 = (bf16[256,3072]{1,0:T(8,128)(2,1)}, f32[16,128]{1,0:T(8,128)}) custom-call(s32[32]{0:T(128)} %order_ref.1, bf16[128,3072]{1,0:T(8,128)(2,1)} %hidden_ref.1, bf16[256,3072]{1,0:T(8,128)(2,1)} %bitcast.6, bf16[128,4096]{1,0:T(8,128)(2,1)} %teacher_hbm.1, f32[16,1,128]{2,1,0:T(1,128)} %bitcast.7), custom_call_target="tpu_custom_call" | custom-call | flops 6442450944 | bytes 6291456 | tf_op jit(solution)/shard_map/pallas_call | solution.py:401
  142.9 0.0 copy-start
  142.9 2.7 %copy.9 = bf16[1,256,3072]{2,1,0:T(8,128)(2,1)} copy(bf16[1,256,3072]{2,1,0:T(8,128)(2,1)} %bitcast.4) | data formatting | bytes 3145728
  145.5 0.0 copy-done
  145.5 0.6 copy.10
Async XLA Ops:
  142.9 2.7 %copy-start = (f32[16,128]{1,0:T(8,128)S(1)}, f32[16,128]{1,0:T(8,128)}, u32[]{:S(2)}) copy-start(f32[16,128]{1,0:T(8,128)} %get-tuple-element.5) | copy-start | bytes 24580

commit v3 on v2

--- a/solution.py
+++ b/solution.py
@@ -17,10 +17,10 @@
     nx, ny, nzh,
     order_ref, hidden_ref, head_hbm, teacher_hbm, weight_ref,
     grad_ref, div_ref,
-    inv, hid, head, tv, tt, rr, qq, ww, tgt, sc, ex, pr,
+    inv, hid, head, tv, tt, picked, qq, ww, tgt, sc, ex, pr,
     src1, ar1, tile2, ar2, tile3, fin,
     csrc1, car1, ctile2, car2, ctile3, cfin,
-    loc, zs, zr, ys, yr, xs, xr, cs, cr, t1s, t1r, t2s, t2r, t3s, t3r, as_, ar_,
+    loc, zs, zr, ys, yr, xs, xr, cs, cr, t2s, t2r, t3s, t3r, as_, ar_,
 ):
     half = ny // 2
     n_dp = 2 * ny
@@ -29,7 +29,7 @@
     me_s = lax.axis_index("dp")
     me_v = lax.axis_index("vocab")
     y, zl = me_s // 2, me_s % 2
-    x, c = me_v // (2 * nzh), me_v % 2
+    x, zh, c = me_v // (2 * nzh), (me_v // 2) % nzh, me_v % 2
     xp = x % 2
     other = 2 * y + 1 - zl
     y_nbr = [{"dp": ((y + 1) % ny) * 2 + zl}, {"dp": ((y + ny - 1) % ny) * 2 + zl}]
@@ -93,6 +93,20 @@
         )
         return 0
 
+    def shift(j):
+        return j // (2 * nzh), (j // 2) % nzh, j % 2
+
+    def moved(j, sign):
+        dx, dz, dc = shift(j)
+        to_x, to_z, to_c = (x + nx + sign * dx) % nx, (zh + nzh + sign * dz) % nzh, (c + dc) % 2
+        to_y, to_l = (y + ny + sign * (2 * dx + dc)) % ny, (zl + dz) % 2
+        return 2 * to_y + to_l, (to_x * nzh + to_z) * 2 + to_c
+
+    def greet_source(j, _):
+        pl.semaphore_signal(barrier, inc=1, device_id=moved(j, -1), device_id_type=MESH)
+        return 0
+
+    lax.fori_loop(1, n_v, greet_source, 0)
     lax.fori_loop(1, n_dp, greet_dp, 0)
     lax.fori_loop(1, n_v, greet_v, 0)
     tload.wait()
@@ -102,25 +116,36 @@
         return 0
 
     lax.fori_loop(0, n_v, flip, 0)
-    pl.semaphore_wait(barrier, n_dp + n_v - 2)
+
+    final = order_ref[me_v]
+
+    def stage_piece(k, _):
+        dx = (final // (2 * nzh) + nx - k // (2 * nzh)) % nx
+        dz = ((final // 2) % nzh + nzh - (k // 2) % nzh) % nzh
+        dc = (final % 2 + k % 2) % 2
+        picked[k] = tt[2 * (2 * ((y + 2 * dx + dc) % ny) + (zl + dz) % 2) + dz // 2]
+        return 0
+
+    lax.fori_loop(0, n_v, stage_piece, 0)
+    pl.semaphore_wait(barrier, n_dp + 2 * n_v - 3)
 
     send(hidden_ref.at[rows(base, 32), :], reg1(me_s, base, 32), zs.at[0], zr.at[0], z_peer)
 
-    def first_rows(g):
-        return (base, 32) if half > 1 else (base + 16 * g, 16)
+    def y_rows(g, d):
+        return (base, 32) if d < half else (base + 16 * g, 16)
 
     for g in range(2):
-        st, ct = first_rows(g)
+        st, ct = y_rows(g, 1)
         send(hidden_ref.at[rows(st, ct), :], reg1(me_s, st, ct),
              ys.at[g, 0], yr.at[g, 0], y_nbr[g])
 
     def t2_step(j, _):
         k = (me_v + j) % n_v
-        send_quiet(tt.at[k], qq.at[me_v], t2s.at[0], t2r.at[0], {"vocab": k})
+        send_quiet(picked.at[k], qq.at[me_v], t2s.at[0], t2r.at[0], {"vocab": k})
         return 0
 
     lax.fori_loop(1, n_v, t2_step, 0)
-    qq[me_v] = tt[me_v]
+    qq[me_v] = picked[me_v]
 
     def inverse_of(v, _):
         found = order_ref[0] * 0
@@ -130,52 +155,18 @@
         return 0
 
     lax.fori_loop(0, n_v, inverse_of, 0)
-    my_pair = me_v // 2
-
     def t3_all():
         wait(qq.at[pl.ds(0, n_v - 1)], t2r.at[0])
 
         def body(j, _):
-            vp = (j + me_s + n_dp - my_pair) % n_dp
-            for cc in range(2):
-                v = 2 * vp + cc
-
-                @pl.when(v != me_v)
-                def _():
-                    ww[v] = qq[inv[v]]
-                    send_quiet(ww.at[v], rr.at[me_v], t3s.at[0], t3r.at[me_v], {"vocab": v})
-
-                @pl.when(v == me_v)
-                def _():
-                    rr[v] = qq[inv[v]]
-
+            to_s, v = moved(j, 1)
+            ww[v] = qq[inv[v]]
+            slot = 2 * me_s + shift(j)[1] // 2
+            send_quiet(ww.at[v], tgt.at[slot], t3s.at[0], t3r.at[0], (to_s, v))
             return 0
 
-        lax.fori_loop(0, n_dp, body, 0)
-
-    def t1_range(lo, hi):
-        def body(j, _):
-            s = (j + me_s + n_dp - my_pair) % n_dp
-            for cc in range(2):
-                k = 2 * s + cc
-
-                @pl.when(k != me_v)
-                def _():
-                    wait(rr.at[k], t3r.at[k])
-
-            @pl.when(s != me_s)
-            def _():
-                send_quiet(rr.at[pl.ds(2 * s, 2)], tgt.at[pl.ds(2 * me_s, 2)],
-                           t1s.at[0], t1r.at[0], {"dp": s})
-
-            @pl.when(s == me_s)
-            def _():
-                tgt[2 * s] = rr[2 * s]
-                tgt[2 * s + 1] = rr[2 * s + 1]
-
-            return 0
-
-        lax.fori_loop(lo, hi, body, 0)
+        lax.fori_loop(1, n_v, body, 0)
+        tgt[2 * me_s] = qq[inv[me_v]]
 
     def teacher_stats():
         def mx(i, acc):
@@ -195,56 +186,60 @@
         d = (idx + 1) // 2
         return (y + ny - d) % ny if idx % 2 == 1 else (y + d) % ny
 
-    def send_x(idx, q):
+    def block_id(g, d):
+        return 2 * d - 1 if g == 0 or d == half else 2 * d
+
+    def shard(idx, j):
         yb = block_y(idx)
-        part = reg1(other, base + 16 * q, 16) if idx == 0 else reg2(yb, base + 16 * q, 16)
-        send(part, part, xs.at[q, idx], xr.at[q, idx], x_nbr[q])
+        return 2 * yb + zl if j == 0 else 2 * yb + 1 - zl
+
+    def send_x(idx, j, q):
+        part = reg1(shard(idx, j), base + 16 * q, 16)
+        k = 2 * idx + j
+        send(part, part, xs.at[q, k], xr.at[q, k], x_nbr[q])
 
     def send_core(idx, kind):
-        yb = block_y(idx)
         st = base if kind == 0 else obase
-        part = reg1(other, st, 32) if idx == 0 else reg2(yb, st, 32)
+        part = reg1(other, st, 32) if idx == 0 else reg2(block_y(idx), st, 32)
         send(part, part, cs.at[kind, idx], cr.at[kind, idx], sib)
 
-    def y_recv(idx):
-        yb = block_y(idx)
-        d = (idx + 1) // 2
-        if idx == 0:
+    def y_recv(d):
+        if d == 0:
             wait(reg1(other, base, 32), zr.at[0])
             for g in range(2):
-                st, ct = first_rows(g)
+                st, ct = y_rows(g, 1)
                 part = reg1(other, st, ct)
                 send(part, part, ys.at[g, 1], yr.at[g, 1], y_nbr[g])
             for q in range(2):
-                send_x(idx, q)
-        elif d < half:
-            g = 0 if idx % 2 == 1 else 1
-            if d == 1:
-                wait(reg1(2 * yb + zl, base, 32), yr.at[g, 0])
-                wait(reg1(2 * yb + 1 - zl, base, 32), yr.at[g, 1])
-            for q in ((0, 1) if g == 0 else (1, 0)):
-                if d > 1:
-                    wait(reg2(yb, base + 16 * q, 16), yr.at[g, 2 * (d - 1) + q])
-                if d + 1 < half or q == g:
-                    part = reg2(yb, base + 16 * q, 16)
-                    send(part, part, ys.at[g, 2 * d + q], yr.at[g, 2 * d + q], y_nbr[g])
-                send_x(idx, q)
-        else:
+                send_x(0, 1, q)
+            send_core(0, 0)
+            return
+        for j in range(2):
             for g in range(2):
-                if d == 1:
-                    wait(reg1(2 * yb + zl, base + 16 * g, 16), yr.at[g, 0])
-                    wait(reg1(2 * yb + 1 - zl, base + 16 * g, 16), yr.at[g, 1])
+                idx = block_id(g, d)
+                st, ct = y_rows(g, d)
+                wait(reg1(shard(idx, j), st, ct), yr.at[g, 2 * (d - 1) + j])
+                if d < half:
+                    st, ct = y_rows(g, d + 1)
+                    part = reg1(shard(idx, j), st, ct)
+                    send(part, part, ys.at[g, 2 * d + j], yr.at[g, 2 * d + j], y_nbr[g])
+                    for q in range(2):
+                        send_x(idx, j, q)
                 else:
-                    wait(reg2(yb, base + 16 * g, 16), yr.at[g, 2 * (d - 1) + g])
-                send_x(idx, g)
-        send_core(idx, 0)
-
-    def x_recv(idx):
-        yb = block_y(idx)
-        for q in range(2):
-            part = reg1(other, obase + 16 * q, 16) if idx == 0 else reg2(yb, obase + 16 * q, 16)
-            wait(part, xr.at[q, idx])
-        send_core(idx, 1)
+                    send_x(idx, j, g)
+        for idx in blocks_at(d):
+            send_core(idx, 0)
+
+    def blocks_at(d):
+        return (0,) if d == 0 else ((2 * d - 1, 2 * d) if d < half else (2 * d - 1,))
+
+    def x_recv(d):
+        for idx in blocks_at(d):
+            for j in range(2):
+                for q in range(2):
+                    if idx > 0 or j > 0:
+                        wait(reg1(shard(idx, j), obase + 16 * q, 16), xr.at[q, 2 * idx + j])
+            send_core(idx, 1)
 
     def compute(idx):
         yb = block_y(idx)
@@ -269,21 +264,18 @@
 
     own.wait()
     hload.wait()
-    t1_plan = {ny - 1: (0, 3), ny: (3, 6), ny + 1: (6, 9)}
-    for stage in range(ny + 2):
-        if stage < ny:
+    for stage in range(half + 3):
+        if stage <= half:
             y_recv(stage)
         if stage == 0:
             teacher_stats()
-        if 1 <= stage <= ny:
+        if 1 <= stage <= half + 1:
             x_recv(stage - 1)
         if stage >= 2:
-            compute(stage - 2)
-        if stage == max(ny - 2, 0):
+            for idx in blocks_at(stage - 2):
+                compute(idx)
+        if stage == half - 1:
             t3_all()
-        if stage in t1_plan:
-            lo, hi = t1_plan[stage]
-            t1_range(min(lo, n_dp), min(hi, n_dp))
 
     def spread_dp(src, dst, k):
         def body(i, _):
@@ -317,18 +309,16 @@
         return top, jnp.sum(sums * jnp.exp(tops - top), axis=0, keepdims=True)
 
     spread_dp(src1, ar1, 0)
-    t1_range(min(9, n_dp), min(12, n_dp))
     wait(ar1.at[pl.ds(0, n_dp - 1)], ar_.at[0])
     tile2[0:1, :], tile2[1:2, :] = merge(ar1, 0)
     share_v(tile2, ar2, 1)
-    t1_range(min(12, n_dp), n_dp)
     wait(ar2.at[pl.ds(0, n_v - 1)], ar_.at[1])
     tile3[0:1, :], tile3[1:2, :] = merge(ar2, 0)
     tile3[2:3, :], tile3[3:4, :] = merge(ar2, 2)
     share_dp(tile3, fin, 2)
     wait(fin.at[pl.ds(0, n_dp - 1)], ar_.at[2])
 
-    wait(tgt.at[pl.ds(0, n_v - 2)], t1r.at[0])
+    wait(tgt.at[pl.ds(0, n_v - 1)], t3r.at[0])
 
     def grad_chunk(s, _):
         cols = pl.ds(pl.multiple_of(s * 128, 128), 128)
@@ -377,8 +367,7 @@
 
     for ref, sem in sent:
         wait(ref, sem)
-    wait(tt.at[pl.ds(0, n_v - 1)], t2s.at[0])
-    wait(rr.at[pl.ds(0, n_v - 2)], t1s.at[0])
+    wait(picked.at[pl.ds(0, n_v - 1)], t2s.at[0])
     wait(ww.at[pl.ds(0, n_v - 1)], t3s.at[0])
     for k, ref in ((0, ar1), (1, ar2), (2, fin), (3, car1), (4, car2), (5, cfin)):
         wait(ref.at[pl.ds(0, (n_v if k % 3 == 1 else n_dp) - 1)], as_.at[k])
@@ -420,11 +409,10 @@
             dma((3,)),
             dma((1,)), dma((1,)),
             dma((2, ny)), dma((2, ny)),
-            dma((2, ny)), dma((2, ny)),
+            dma((2, 2 * ny)), dma((2, 2 * ny)),
             dma((2, ny)), dma((2, ny)),
             dma((1,)), dma((1,)),
             dma((1,)), dma((1,)),
-            dma((1,)), dma((n_v,)),
             dma((6,)), dma((6,)),
         ],
         compiler_params=pltpu.CompilerParams(

time: 146 us -> 123 us (0.84)
  Pallas kernels: 142 us -> 119 us
    pallas_call x1, Pallas kernels: 142 us -> 119 us  [on_device(): pl.pallas_call(functools.partial(kernel, nx, ny, nzh), out_shape=(jax.Sha...]
where the time goes in v3:
time: 123 us
  Pallas kernels  119 us (97%)
  local copies, waits for them, and re-layouts  3.26 us (3%)
    pallas_call x1, Pallas kernels, on_device(): pl.pallas_call(functools.partial(kernel, nx, ny, nzh), out_shape=(jax.Sha...  119 us
    unnamed x4, local copies, waits for them, and re-layouts  3.26 us

profile of v3, /device:TPU:1, one launch (start us, length us, event | category | flops | bytes accessed | tf_op | source)
XLA Modules:
  0.0 123.0 jit_solution(3044337414159366384)
XLA Ops:
  0.6 119.1 %shard_map.68 = (bf16[256,3072]{1,0:T(8,128)(2,1)}, f32[16,128]{1,0:T(8,128)}) custom-call(s32[32]{0:T(128)} %order_ref.1, bf16[128,3072]{1,0:T(8,128)(2,1)} %hidden_ref.1, bf16[256,3072]{1,0:T(8,128)(2,1)} %bitcast.6, bf16[128,4096]{1,0:T(8,128)(2,1)} %teacher_hbm.1, f32[16,1,128]{2,1,0:T(1,128)} %bitcast.7), custom_call_target="tpu_custom_call" | custom-call | flops 6442450944 | bytes 6291456 | tf_op jit(solution)/shard_map/pallas_call | solution.py:390
  119.7 0.0 copy-start
  119.7 2.7 %copy.9 = bf16[1,256,3072]{2,1,0:T(8,128)(2,1)} copy(bf16[1,256,3072]{2,1,0:T(8,128)(2,1)} %bitcast.4) | data formatting | bytes 3145728
  122.4 0.0 copy-done
  122.4 0.6 copy.10
Async XLA Ops:
  119.7 2.7 %copy-start = (f32[16,128]{1,0:T(8,128)S(1)}, f32[16,128]{1,0:T(8,128)}, u32[]{:S(2)}) copy-start(f32[16,128]{1,0:T(8,128)} %get-tuple-element.5) | copy-start | bytes 24580

commit v4 on v3

--- a/solution.py
+++ b/solution.py
@@ -13,11 +13,19 @@
 SUB = 256
 
 
+def rem(a, b):
+    return lax.rem(a, jnp.int32(b))
+
+
+def div(a, b):
+    return lax.div(a, jnp.int32(b))
+
+
 def kernel(
     nx, ny, nzh,
     order_ref, hidden_ref, head_hbm, teacher_hbm, weight_ref,
     grad_ref, div_ref,
-    inv, hid, head, tv, tt, picked, qq, ww, tgt, sc, ex, pr,
+    inv, hid, head, tv, tt, picked, qq, ww, tgt, sc, ex, et, pr,
     src1, ar1, tile2, ar2, tile3, fin,
     csrc1, car1, ctile2, car2, ctile3, cfin,
     loc, zs, zr, ys, yr, xs, xr, cs, cr, t2s, t2r, t3s, t3r, as_, ar_,
@@ -28,14 +36,14 @@
     d_model = hid.shape[-1]
     me_s = lax.axis_index("dp")
     me_v = lax.axis_index("vocab")
-    y, zl = me_s // 2, me_s % 2
-    x, zh, c = me_v // (2 * nzh), (me_v // 2) % nzh, me_v % 2
-    xp = x % 2
+    y, zl = div(me_s, 2), rem(me_s, 2)
+    x, zh, c = div(me_v, 2 * nzh), rem(div(me_v, 2), nzh), rem(me_v, 2)
+    xp = rem(x, 2)
     other = 2 * y + 1 - zl
-    y_nbr = [{"dp": ((y + 1) % ny) * 2 + zl}, {"dp": ((y + ny - 1) % ny) * 2 + zl}]
+    y_nbr = [{"dp": rem(y + 1, ny) * 2 + zl}, {"dp": rem(y + ny - 1, ny) * 2 + zl}]
     x_nbr = [
-        {"vocab": ((x + 1) % nx) * (2 * nzh) + me_v % (2 * nzh)},
-        {"vocab": ((x + nx - 1) % nx) * (2 * nzh) + me_v % (2 * nzh)},
+        {"vocab": rem(x + 1, nx) * (2 * nzh) + rem(me_v, 2 * nzh)},
+        {"vocab": rem(x + nx - 1, nx) * (2 * nzh) + rem(me_v, 2 * nzh)},
     ]
     sib = {"vocab": me_v + 1 - 2 * c}
     z_peer = {"dp": other}
@@ -83,23 +91,23 @@
 
     def greet_dp(i, _):
         pl.semaphore_signal(
-            barrier, inc=1, device_id={"dp": (me_s + i) % n_dp}, device_id_type=MESH
+            barrier, inc=1, device_id={"dp": rem(me_s + i, n_dp)}, device_id_type=MESH
         )
         return 0
 
     def greet_v(i, _):
         pl.semaphore_signal(
-            barrier, inc=1, device_id={"vocab": (me_v + i) % n_v}, device_id_type=MESH
+            barrier, inc=1, device_id={"vocab": rem(me_v + i, n_v)}, device_id_type=MESH
         )
         return 0
 
     def shift(j):
-        return j // (2 * nzh), (j // 2) % nzh, j % 2
+        return div(j, 2 * nzh), rem(div(j, 2), nzh), rem(j, 2)
 
     def moved(j, sign):
         dx, dz, dc = shift(j)
-        to_x, to_z, to_c = (x + nx + sign * dx) % nx, (zh + nzh + sign * dz) % nzh, (c + dc) % 2
-        to_y, to_l = (y + ny + sign * (2 * dx + dc)) % ny, (zl + dz) % 2
+        to_x, to_z, to_c = rem(x + nx + sign * dx, nx), rem(zh + nzh + sign * dz, nzh), rem(c + dc, 2)
+        to_y, to_l = rem(y + ny + sign * (2 * dx + dc), ny), rem(zl + dz, 2)
         return 2 * to_y + to_l, (to_x * nzh + to_z) * 2 + to_c
 
     def greet_source(j, _):
@@ -120,10 +128,10 @@
     final = order_ref[me_v]
 
     def stage_piece(k, _):
-        dx = (final // (2 * nzh) + nx - k // (2 * nzh)) % nx
-        dz = ((final // 2) % nzh + nzh - (k // 2) % nzh) % nzh
-        dc = (final % 2 + k % 2) % 2
-        picked[k] = tt[2 * (2 * ((y + 2 * dx + dc) % ny) + (zl + dz) % 2) + dz // 2]
+        dx = rem(div(final, 2 * nzh) + nx - div(k, 2 * nzh), nx)
+        dz = rem(rem(div(final, 2), nzh) + nzh - rem(div(k, 2), nzh), nzh)
+        dc = rem(rem(final, 2) + rem(k, 2), 2)
+        picked[k] = tt[2 * (2 * rem(y + 2 * dx + dc, ny) + rem(zl + dz, 2)) + div(dz, 2)]
         return 0
 
     lax.fori_loop(0, n_v, stage_piece, 0)
@@ -140,7 +148,7 @@
              ys.at[g, 0], yr.at[g, 0], y_nbr[g])
 
     def t2_step(j, _):
-        k = (me_v + j) % n_v
+        k = rem(me_v + j, n_v)
         send_quiet(picked.at[k], qq.at[me_v], t2s.at[0], t2r.at[0], {"vocab": k})
         return 0
 
@@ -161,7 +169,7 @@
         def body(j, _):
             to_s, v = moved(j, 1)
             ww[v] = qq[inv[v]]
-            slot = 2 * me_s + shift(j)[1] // 2
+            slot = 2 * me_s + div(shift(j)[1], 2)
             send_quiet(ww.at[v], tgt.at[slot], t3s.at[0], t3r.at[0], (to_s, v))
             return 0
 
@@ -184,7 +192,7 @@
 
     def block_y(idx):
         d = (idx + 1) // 2
-        return (y + ny - d) % ny if idx % 2 == 1 else (y + d) % ny
+        return rem(y + ny - d, ny) if idx % 2 == 1 else rem(y + d, ny)
 
     def block_id(g, d):
         return 2 * d - 1 if g == 0 or d == half else 2 * d
@@ -279,7 +287,7 @@
 
     def spread_dp(src, dst, k):
         def body(i, _):
-            s = (me_s + i) % n_dp
+            s = rem(me_s + i, n_dp)
             send_quiet(src.at[s], dst.at[me_s], as_.at[k], ar_.at[k], {"dp": s})
             return 0
 
@@ -288,7 +296,7 @@
 
     def share_v(tile, dst, k):
         def body(i, _):
-            send_quiet(tile, dst.at[me_v], as_.at[k], ar_.at[k], {"vocab": (me_v + i) % n_v})
+            send_quiet(tile, dst.at[me_v], as_.at[k], ar_.at[k], {"vocab": rem(me_v + i, n_v)})
             return 0
 
         lax.fori_loop(1, n_v, body, 0)
@@ -296,7 +304,7 @@
 
     def share_dp(tile, dst, k):
         def body(i, _):
-            send_quiet(tile, dst.at[me_s], as_.at[k], ar_.at[k], {"dp": (me_s + i) % n_dp})
+            send_quiet(tile, dst.at[me_s], as_.at[k], ar_.at[k], {"dp": rem(me_s + i, n_dp)})
             return 0
 
         lax.fori_loop(1, n_dp, body, 0)
@@ -308,17 +316,19 @@
         top = jnp.max(tops, axis=0, keepdims=True)
         return top, jnp.sum(sums * jnp.exp(tops - top), axis=0, keepdims=True)
 
-    spread_dp(src1, ar1, 0)
-    wait(ar1.at[pl.ds(0, n_dp - 1)], ar_.at[0])
-    tile2[0:1, :], tile2[1:2, :] = merge(ar1, 0)
-    share_v(tile2, ar2, 1)
-    wait(ar2.at[pl.ds(0, n_v - 1)], ar_.at[1])
-    tile3[0:1, :], tile3[1:2, :] = merge(ar2, 0)
-    tile3[2:3, :], tile3[3:4, :] = merge(ar2, 2)
-    share_dp(tile3, fin, 2)
-    wait(fin.at[pl.ds(0, n_dp - 1)], ar_.at[2])
-
-    wait(tgt.at[pl.ds(0, n_v - 1)], t3r.at[0])
+    def target_chunk(s, _):
+        cols = pl.ds(pl.multiple_of(s * 128, 128), 128)
+        t = [tgt[2 * s + h].astype(F32) for h in range(2)]
+        top = jnp.max(jnp.maximum(t[0], t[1]), axis=0, keepdims=True)
+        cross = jnp.zeros((1, 128), F32)
+        for h in range(2):
+            band = slice(128 * h, 128 * h + 128)
+            e_t = jnp.exp(t[h] - top)
+            et[band, cols] = e_t
+            cross = cross + jnp.sum(e_t * (t[h] - sc[band, cols]), axis=0, keepdims=True)
+        csrc1[s, 0:1, :] = top
+        csrc1[s, 1:2, :] = cross
+        return 0
 
     def grad_chunk(s, _):
         cols = pl.ds(pl.multiple_of(s * 128, 128), 128)
@@ -326,18 +336,11 @@
         m_s, z_s, m_t, z_t = f[0:1], f[1:2], f[2:3], f[3:4]
         w = weight_ref[s]
         scale_s = w * jnp.exp(src1[s][0:1] - m_s) / z_s
-        scale_t = w / z_t
-        cross = jnp.zeros((1, 128), F32)
+        scale_t = w * jnp.exp(csrc1[s][0:1] - m_t) / z_t
         for h in range(2):
-            t = tgt[2 * s + h].astype(F32)
-            e_t = jnp.exp(t - m_t)
             band = slice(128 * h, 128 * h + 128)
-            cross = cross + jnp.sum(e_t * (t - sc[band, cols]), axis=0, keepdims=True)
-            pr[band, cols] = (ex[band, cols] * scale_s - e_t * scale_t).astype(BF16)
-        csrc1[s] = cross
-        return 0
-
-    lax.fori_loop(0, n_dp, grad_chunk, 0)
+            pr[band, cols] = (ex[band, cols] * scale_s - et[band, cols] * scale_t).astype(BF16)
+        return 0
 
     n_tiles = d_model // 256
 
@@ -350,20 +353,31 @@
 
         lax.fori_loop(lo, hi, body, 0)
 
-    cut1, cut2 = n_tiles // 3, 2 * n_tiles // 3
+    spread_dp(src1, ar1, 0)
+    wait(ar1.at[pl.ds(0, n_dp - 1)], ar_.at[0])
+    tile2[0:1, :], tile2[1:2, :] = merge(ar1, 0)
+    share_v(tile2, ar2, 1)
+    wait(tgt.at[pl.ds(0, n_v - 1)], t3r.at[0])
+    lax.fori_loop(0, n_dp, target_chunk, 0)
     spread_dp(csrc1, car1, 3)
-    gemm(0, cut1)
+    wait(ar2.at[pl.ds(0, n_v - 1)], ar_.at[1])
+    tile3[0:1, :], tile3[1:2, :] = merge(ar2, 0)
+    tile3[2:3, :], tile3[3:4, :] = merge(ar2, 2)
+    share_dp(tile3, fin, 2)
     wait(car1.at[pl.ds(0, n_dp - 1)], ar_.at[3])
-    ctile2[...] = jnp.sum(car1[...], axis=0)
+    ctile2[0:1, :], ctile2[1:2, :] = merge(car1, 0)
     share_v(ctile2, car2, 4)
-    gemm(cut1, cut2)
+    wait(fin.at[pl.ds(0, n_dp - 1)], ar_.at[2])
+    lax.fori_loop(0, n_dp, grad_chunk, 0)
+    cut = n_tiles // 3
+    gemm(0, cut)
     wait(car2.at[pl.ds(0, n_v - 1)], ar_.at[4])
-    ctile3[...] = jnp.sum(car2[...], axis=0)
+    ctile3[0:1, :], ctile3[1:2, :] = merge(car2, 0)
     share_dp(ctile3, cfin, 5)
-    gemm(cut2, n_tiles)
+    gemm(cut, n_tiles)
     wait(cfin.at[pl.ds(0, n_dp - 1)], ar_.at[5])
     m_s, z_s, m_t, z_t = fin[:, 0, :], fin[:, 1, :], fin[:, 2, :], fin[:, 3, :]
-    div_ref[...] = cfin[:, 0, :] / z_t - m_t - jnp.log(z_t) + m_s + jnp.log(z_s)
+    div_ref[...] = cfin[:, 1, :] / z_t - m_t - jnp.log(z_t) + m_s + jnp.log(z_s)
 
     for ref, sem in sent:
         wait(ref, sem)
@@ -385,7 +399,7 @@
     def stat(n, r):
         return pltpu.VMEM((n, r, 128), F32)
 
-    tile4, tile1 = pltpu.VMEM((4, 128), F32), pltpu.VMEM((1, 128), F32)
+    tile4, tile2 = pltpu.VMEM((4, 128), F32), pltpu.VMEM((2, 128), F32)
     pieces = pltpu.VMEM((n_v, 128, 128), BF16)
     grad, div = pl.pallas_call(
         functools.partial(kernel, nx, ny, nzh),
@@ -403,9 +417,10 @@
             pieces, pieces, pieces, pieces, pieces,
             pltpu.VMEM((SUB, tokens), F32),
             pltpu.VMEM((SUB, tokens), F32),
+            pltpu.VMEM((SUB, tokens), F32),
             pltpu.VMEM((SUB, tokens), BF16),
             stat(n_dp, 2), stat(n_dp, 2), tile4, stat(n_v, 4), tile4, stat(n_dp, 4),
-            stat(n_dp, 1), stat(n_dp, 1), tile1, stat(n_v, 1), tile1, stat(n_dp, 1),
+            stat(n_dp, 2), stat(n_dp, 2), tile2, stat(n_v, 2), tile2, stat(n_dp, 2),
             dma((3,)),
             dma((1,)), dma((1,)),
             dma((2, ny)), dma((2, ny)),

time: 123 us -> 114 us (0.927)
  Pallas kernels: 119 us -> 110 us
    pallas_call x1, Pallas kernels: 119 us -> 110 us  [on_device(): pl.pallas_call(functools.partial(kernel, nx, ny, nzh), out_shape=(jax.Sha...]
where the time goes in v4:
time: 114 us
  Pallas kernels  110 us (96%)
  local copies, waits for them, and re-layouts  3.26 us (3%)
    pallas_call x1, Pallas kernels, on_device(): pl.pallas_call(functools.partial(kernel, nx, ny, nzh), out_shape=(jax.Sha...  110 us
    unnamed x4, local copies, waits for them, and re-layouts  3.26 us

profile of v4, /device:TPU:1, one launch (start us, length us, event | category | flops | bytes accessed | tf_op | source)
XLA Modules:
  0.0 114.1 jit_solution(12512368410831654203)
XLA Ops:
  0.6 110.2 %shard_map.68 = (bf16[256,3072]{1,0:T(8,128)(2,1)}, f32[16,128]{1,0:T(8,128)}) custom-call(s32[32]{0:T(128)} %order_ref.1, bf16[128,3072]{1,0:T(8,128)(2,1)} %hidden_ref.1, bf16[256,3072]{1,0:T(8,128)(2,1)} %bitcast.6, bf16[128,4096]{1,0:T(8,128)(2,1)} %teacher_hbm.1, f32[16,1,128]{2,1,0:T(1,128)} %bitcast.7), custom_call_target="tpu_custom_call" | custom-call | flops 6442450944 | bytes 6291456 | tf_op jit(solution)/shard_map/pallas_call | solution.py:404
  110.8 0.0 copy-start
  110.8 2.7 %copy.9 = bf16[1,256,3072]{2,1,0:T(8,128)(2,1)} copy(bf16[1,256,3072]{2,1,0:T(8,128)(2,1)} %bitcast.4) | data formatting | bytes 3145728
  113.5 0.0 copy-done
  113.5 0.6 copy.10
Async XLA Ops:
  110.8 2.7 %copy-start = (f32[16,128]{1,0:T(8,128)S(1)}, f32[16,128]{1,0:T(8,128)}, u32[]{:S(2)}) copy-start(f32[16,128]{1,0:T(8,128)} %get-tuple-element.5) | copy-start | bytes 24580

commit v5 on v4

--- a/solution.py
+++ b/solution.py
@@ -11,6 +11,7 @@
 BF16 = jnp.bfloat16
 MESH = pl.DeviceIdType.MESH
 SUB = 256
+HANDOVERS = 2
 
 
 def rem(a, b):
@@ -152,8 +153,6 @@
         send_quiet(picked.at[k], qq.at[me_v], t2s.at[0], t2r.at[0], {"vocab": k})
         return 0
 
-    lax.fori_loop(1, n_v, t2_step, 0)
-    qq[me_v] = picked[me_v]
 
     def inverse_of(v, _):
         found = order_ref[0] * 0
@@ -276,7 +275,8 @@
         if stage <= half:
             y_recv(stage)
         if stage == 0:
-            teacher_stats()
+            lax.fori_loop(1, n_v, t2_step, 0)
+            qq[me_v] = picked[me_v]
         if 1 <= stage <= half + 1:
             x_recv(stage - 1)
         if stage >= 2:
@@ -284,6 +284,7 @@
                 compute(idx)
         if stage == half - 1:
             t3_all()
+            teacher_stats()
 
     def spread_dp(src, dst, k):
         def body(i, _):
@@ -385,6 +386,11 @@
     wait(ww.at[pl.ds(0, n_v - 1)], t3s.at[0])
     for k, ref in ((0, ar1), (1, ar2), (2, fin), (3, car1), (4, car2), (5, cfin)):
         wait(ref.at[pl.ds(0, (n_v if k % 3 == 1 else n_dp) - 1)], as_.at[k])
+
+
+def hand_over(grad_ref, div_ref, grad_out, div_out):
+    grad_out[...] = grad_ref[...]
+    div_out[...] = div_ref[...]
 
 
 def on_device(nx, ny, nzh, hidden, head, teacher, shard_order, loss_weight):
@@ -437,6 +443,18 @@
             flops=4 * SUB * tokens * d_model, bytes_accessed=8 * SUB * d_model, transcendentals=0
         ),
     )(shard_order, hidden, head[0], teacher, loss_weight.reshape(n_dp, 1, 128))
+    band = pl.BlockSpec((SUB // HANDOVERS, d_model), lambda i: (i, 0))
+    whole = pl.BlockSpec((n_dp, 128), lambda i: (0, 0))
+    grad, div = pl.pallas_call(
+        hand_over,
+        grid=(HANDOVERS,),
+        out_shape=(
+            jax.ShapeDtypeStruct((SUB, d_model), BF16),
+            jax.ShapeDtypeStruct((n_dp, 128), F32),
+        ),
+        in_specs=[band, whole],
+        out_specs=(band, whole),
+    )(grad, div)
     return grad[None], div.reshape(tokens)
 
 

time: 114 us -> 112 us (0.982)
  local copies, waits for them, and re-layouts: 3.26 us -> 0 us
    unnamed x4 -> x0, local copies, waits for them, and re-layouts: 3.26 us -> none
    pallas_call x0 -> x1, Pallas kernels: none -> 2.34 us  [on_device(): pl.pallas_call(hand_over, grid=(HANDOVERS,), out_shape=(jax.ShapeDtypeStr...]
    pallas_call x1, Pallas kernels: 110 us -> 109 us  [on_device(): pl.pallas_call(functools.partial(kernel, nx, ny, nzh), out_shape=(jax.Sha...]
where the time goes in v5:
time: 112 us
  Pallas kernels  111 us (99%)
    pallas_call x1, Pallas kernels, on_device(): pl.pallas_call(functools.partial(kernel, nx, ny, nzh), out_shape=(jax.Sha...  109 us
    pallas_call x1, Pallas kernels, on_device(): pl.pallas_call(hand_over, grid=(HANDOVERS,), out_shape=(jax.ShapeDtypeStr...  2.34 us

profile of v5, /device:TPU:1, one launch (start us, length us, event | category | flops | bytes accessed | tf_op | source)
XLA Modules:
  0.0 112.0 jit_solution(7288429079093425542)
XLA Ops:
  0.6 109.0 %shard_map.68 = (bf16[256,3072]{1,0:T(8,128)(2,1)}, f32[16,128]{1,0:T(8,128)}) custom-call(s32[32]{0:T(128)} %order_ref.1, bf16[128,3072]{1,0:T(8,128)(2,1)} %hidden_ref.1, bf16[256,3072]{1,0:T(8,128)(2,1)} %bitcast.4, bf16[128,4096]{1,0:T(8,128)(2,1)} %teacher_hbm.1, f32[16,1,128]{2,1,0:T(1,128)} %bitcast.6), custom_call_target="tpu_custom_call" | custom-call | flops 6442450944 | bytes 6291456 | tf_op jit(solution)/shard_map/pallas_call | solution.py:410
  109.6 2.3 %shard_map.69 = (bf16[256,3072]{1,0:T(8,128)(2,1)}, f32[16,128]{1,0:T(8,128)}) custom-call(bf16[256,3072]{1,0:T(8,128)(2,1)} %get-tuple-element.6.grad_ref, f32[16,128]{1,0:T(8,128)} %get-tuple-element.7.div_ref), custom_call_target="tpu_custom_call" | custom-call | tf_op jit(solution)/shard_map/pallas_call | solution.py:448

commit v6 on v5

--- a/solution.py
+++ b/solution.py
@@ -148,11 +148,20 @@
         send(hidden_ref.at[rows(st, ct), :], reg1(me_s, st, ct),
              ys.at[g, 0], yr.at[g, 0], y_nbr[g])
 
-    def t2_step(j, _):
-        k = rem(me_v + j, n_v)
+    def t2_send(m, dz):
+        to_x, to_z, to_c = rem(x + div(m, 2), nx), rem(zh + dz, nzh), rem(c + rem(m, 2), 2)
+        k = (to_x * nzh + to_z) * 2 + to_c
         send_quiet(picked.at[k], qq.at[me_v], t2s.at[0], t2r.at[0], {"vocab": k})
-        return 0
-
+
+    def t2_near(m, _):
+        t2_send(m, 0)
+        return 0
+
+    def t2_far(i, _):
+        t2_send(rem(i, 2 * nx), 1 + div(i, 2 * nx))
+        return 0
+
+    lax.fori_loop(1, 2 * nx, t2_near, 0)
 
     def inverse_of(v, _):
         found = order_ref[0] * 0
@@ -275,7 +284,7 @@
         if stage <= half:
             y_recv(stage)
         if stage == 0:
-            lax.fori_loop(1, n_v, t2_step, 0)
+            lax.fori_loop(0, 2 * nx * (nzh - 1), t2_far, 0)
             qq[me_v] = picked[me_v]
         if 1 <= stage <= half + 1:
             x_recv(stage - 1)

time: 112 us -> 109 us (0.973)
  Pallas kernels: 111 us -> 108 us
    pallas_call x1, Pallas kernels: 109 us -> 106 us  [on_device(): pl.pallas_call(functools.partial(kernel, nx, ny, nzh), out_shape=(jax.Sha...]
where the time goes in v6:
time: 109 us
  Pallas kernels  108 us (99%)
    pallas_call x1, Pallas kernels, on_device(): pl.pallas_call(functools.partial(kernel, nx, ny, nzh), out_shape=(jax.Sha...  106 us
    pallas_call x1, Pallas kernels, on_device(): pl.pallas_call(hand_over, grid=(HANDOVERS,), out_shape=(jax.ShapeDtypeStr...  2.34 us

profile of v6, /device:TPU:1, one launch (start us, length us, event | category | flops | bytes accessed | tf_op | source)
XLA Modules:
  0.0 108.5 jit_solution(13388898582680226798)
XLA Ops:
  0.6 105.6 %shard_map.68 = (bf16[256,3072]{1,0:T(8,128)(2,1)}, f32[16,128]{1,0:T(8,128)}) custom-call(s32[32]{0:T(128)} %order_ref.1, bf16[128,3072]{1,0:T(8,128)(2,1)} %hidden_ref.1, bf16[256,3072]{1,0:T(8,128)(2,1)} %bitcast.4, bf16[128,4096]{1,0:T(8,128)(2,1)} %teacher_hbm.1, f32[16,1,128]{2,1,0:T(1,128)} %bitcast.6), custom_call_target="tpu_custom_call" | custom-call | flops 6442450944 | bytes 6291456 | tf_op jit(solution)/shard_map/pallas_call | solution.py:419
  106.2 2.3 %shard_map.69 = (bf16[256,3072]{1,0:T(8,128)(2,1)}, f32[16,128]{1,0:T(8,128)}) custom-call(bf16[256,3072]{1,0:T(8,128)(2,1)} %get-tuple-element.6.grad_ref, f32[16,128]{1,0:T(8,128)} %get-tuple-element.7.div_ref), custom_call_target="tpu_custom_call" | custom-call | tf_op jit(solution)/shard_map/pallas_call | solution.py:457
